TPU v7x, 256 devices: a whole 4x4x8 slice. The times are simulated.
256 devices in a mesh: dp: 8 (over z_hi, y), segment: 32 (over z_lo, x, core).
Axes of the slice: x: 4, y: 4, z: 8 (z_hi: 2, z_lo: 4; z = z_hi * 4 + z_lo), core: 2. Of those that a mesh axis runs over, the one named last changes fastest.
Arguments:
- hidden_rows: float32 [4096, 2048], P('dp', 'segment'), may hold values from -10 to 10
- norm_gain: float32 [2048], replicated, may hold values from 0.25 to 1.75
- head_weight: bfloat16 [2048, 77824], P(None, 'segment'), may hold values from -1 to 1
- teacher_ids: int32 [4096, 32], P('dp'), may hold values from 0 to 77823, as said below
- teacher_logits: float32 [4096, 32], P('dp'), may hold values from -20 to 460
- token_weights: float32 [4096], P('dp'), may hold values from 0.5 to 10, as said below
Outputs:
- token_loss: float32 [4096], P('dp')
- mean_loss: float32 [], replicated
- grad_rows: float32 [4096, 2048], P('dp', 'segment')
Inputs may be any that keep to these rules, and one draw needn't show every extreme that they name: `teacher_ids`: each row holds 32 different vocabulary indices. `token_weights`: positive.
All inputs are finite; a program needn't handle non-finite values.
Results may differ from a plain program's by a relative error of at most 0.0078.
Values may be sent and summed in bfloat16 or wider, within the bound.
A program may use at most 64 MiB of HBM per device.

v0:
```python
import jax
import jax.numpy as jnp
from jax import lax
from jax.sharding import PartitionSpec as P

D = 2048


EPSILON = 1e-06


def owned_targets(local_ids, teacher_prob, logits):
    token_count, vocab_share = logits.shape
    block_rows = 128
    block_count = token_count // block_rows
    columns = jnp.arange(vocab_share, dtype=jnp.int32)

    def one_block(inputs):
        id_block, prob_block, logit_block = inputs
        matches = id_block[:, :, None] == columns[None, None, :]
        target_block = jnp.sum(jnp.where(matches, prob_block[:, :, None], 0.0), axis=1)
        return (target_block, jnp.sum(target_block * logit_block, axis=1))

    targets, weighted_pick = lax.map(
        one_block,
        (
            local_ids.reshape(block_count, block_rows, -1),
            teacher_prob.reshape(block_count, block_rows, -1),
            logits.reshape(block_count, block_rows, vocab_share),
        ),
    )
    return (targets.reshape(token_count, vocab_share), weighted_pick.reshape(token_count))


def shards(hidden_rows, norm_gain, head_weight, teacher_ids, teacher_logits, token_weights):
    segment_index = lax.axis_index("segment")
    token_count = hidden_rows.shape[0]
    width_share = hidden_rows.shape[1]
    vocab_share = head_weight.shape[1]
    vocab_start = segment_index * vocab_share
    all_tokens = token_count * lax.axis_size("dp")
    gain_share = lax.dynamic_slice_in_dim(norm_gain, segment_index * width_share, width_share, 0)
    whole_rows = lax.all_gather(hidden_rows, "segment", axis=1, tiled=True)
    squares = jnp.sum(whole_rows * whole_rows, axis=1)
    inverse_rms = lax.rsqrt(squares / D + EPSILON)
    normed = (whole_rows * inverse_rms[:, None] * norm_gain[None, :]).astype(jnp.bfloat16)
    logits = jnp.dot(normed, head_weight, preferred_element_type=jnp.float32)
    teacher_max = jnp.max(teacher_logits, axis=1, keepdims=True)
    shifted = teacher_logits - teacher_max
    teacher_logq = shifted - jnp.log(jnp.sum(jnp.exp(shifted), axis=1, keepdims=True))
    teacher_prob = jnp.exp(teacher_logq)
    local_ids = teacher_ids - vocab_start
    targets, weighted_pick = owned_targets(local_ids, teacher_prob, logits)
    local_max = jnp.max(logits, axis=1)
    row_max = lax.pmax(local_max, "segment")
    local_sum = jnp.sum(jnp.exp(logits - row_max[:, None]), axis=1)
    exp_total, pick_total = lax.psum((local_sum, weighted_pick), "segment")
    log_total = row_max + jnp.log(exp_total)
    token_loss = jnp.sum(teacher_prob * teacher_logq, axis=1) - pick_total + log_total
    local_loss = jnp.sum(token_weights * token_loss)
    weight_total, loss_total = lax.psum((jnp.sum(token_weights), local_loss), "dp")
    mean_loss = loss_total / weight_total
    coefficient = token_weights * all_tokens / weight_total
    grad_logits = (coefficient[:, None] * (jnp.exp(logits - log_total[:, None]) - targets)).astype(
        jnp.bfloat16
    )
    grad_share = lax.psum_scatter(
        lax.dot_general(
            head_weight, grad_logits, (((1,), (1,)), ((), ())), preferred_element_type=jnp.float32
        ),
        "segment",
        scatter_dimension=0,
        tiled=True,
    ).T
    scaled = grad_share * gain_share[None, :]
    dot_total = lax.psum(jnp.sum(scaled * hidden_rows, axis=1), "segment")
    grad_rows = inverse_rms[:, None] * (
        scaled - hidden_rows * (inverse_rms * inverse_rms * dot_total / D)[:, None]
    )
    return (token_loss, mean_loss, grad_rows)


def solution(mesh):
    in_specs = (P("dp", "segment"), P(), P(None, "segment"), P("dp", None), P("dp", None), P("dp"))
    out_specs = (P("dp"), P(), P("dp", "segment"))
    return jax.shard_map(shards, mesh=mesh, in_specs=in_specs, out_specs=out_specs, check_vma=False)
```

profile of v0, /device:TPU:8, one launch (start us, length us, event | category | flops | bytes accessed | tf_op | source)
XLA Modules:
  0.0 552.0 jit_solution(1969572167940308506)
XLA Ops:
  7.2 0.0 copy-start.2
  7.2 0.0 all-gather.2.cloned.1.call-start
  7.2 0.7 all-gather.2.cloned.1.call-update
  7.9 0.0 reduce-scatter.4.cloned.1.call-start
  8.0 0.9 reduce_max.18
  8.8 0.9 exponential_reduce_fusion.1
  9.7 0.9 subtract_exponential_fusion
  10.6 0.1 copy.20
  10.7 0.8 broadcast_subtract_fusion
  11.6 0.1 copy.19
  11.7 63.9 %all-gather.2.cloned.1.call-done = f32[512,2048]{0,1:T(8,128)} async-done(((f32[512,64]{0,1:T(8,128)}), f32[512,2048]{0,1:T(8,128)}) %all-gather.2.cloned.1.call-update) | async-done | bytes 4194320 | tf_op jit(solution)/shard_map/all_gather | solution.py:43
  75.6 2.5 multiply_reduce_fusion
  78.2 0.0 copy-done.2
  78.2 12.0 %fusion.11 = (f32[512]{0:T(512)S(1)}, f32[512,2432]{1,0:T(8,128)}) fusion(bf16[2048,2432]{1,0:T(8,128)(2,1)} %param.10, f32[512,2048]{0,1:T(8,128)} %all-gather.2.cloned.1.call-done, f32[2048]{0:T(1024)S(1)} %copy-done.2, f32[512]{0:T(512)S(1)} %add_rsqrt_fusion), kind=kOutput, calls=%fused_computation.33 | convolution fusion | flops 5104664064 | bytes 19148800 | tf_op jit(solution)/shard_map/dot_general | solution.py:47
  90.2 70.5 %pmax.7 = f32[512]{0:T(512)S(1)} all-reduce(f32[512]{0:T(512)S(1)} %get-tuple-element.88), channel_id=1, replica_groups=mesh['dp'=8,'segment'=32] {'segment'}, use_global_device_ids=true, to_apply=%region_10.11 | all-reduce | flops 512 | bytes 4096 | tf_op jit(solution)/shard_map/pmax | solution.py:55
  160.7 3.2 exponential_reduce_fusion
  163.9 0.0 copy-start.1
  163.9 47.1 %while.13 = (s32[]{:T(128)}, f32[4,128,2432]{2,1,0:T(8,128)}, f32[4,128]{1,0:T(4,128)S(1)}, s32[4,128,32]{2,1,0:T(8,128)S(1)}, f32[4,128,32]{2,1,0:T(8,128)S(1)}...) while((s32[]{:T(128)}, f32[4,128,2432]{2,1,0:T(8,128)}, f32[4,128]{1,0:T(4,128)S(1)}, ...), condition=%wide.region_7.8_spmd.clone, body=%wide.region_4.7_spmd.clone.sunk | while | flops 30195584 | bytes 6326373 | solution.py:24
  164.0 9.0 %select_reduce_fusion.2 = f32[128,2432]{1,0:T(8,128)S(1)} fusion(f32[128,32]{1,0:T(8,128)S(1)} %dynamic-slice_bitcast_fusion.4, s32[128,32]{1,0:T(8,128)S(1)} %dynamic-slice_bitcast_fusion.5), kind=kLoop, calls=%fused_computation.2.clone.1 | loop fusion | flops 29573120 | bytes 1277952 | tf_op jit(solution)/shard_map/while/body/eval_jaxpr/reduce_sum | solution.py:21
  173.0 1.5 fusion.16
  174.6 1.1 bitcast_dynamic-update-slice_fusion.2
  175.7 9.0 %select_reduce_fusion.2 = f32[128,2432]{1,0:T(8,128)S(1)} fusion(f32[128,32]{1,0:T(8,128)S(1)} %dynamic-slice_bitcast_fusion.4, s32[128,32]{1,0:T(8,128)S(1)} %dynamic-slice_bitcast_fusion.5), kind=kLoop, calls=%fused_computation.2.clone.1 | loop fusion | flops 29573120 | bytes 1277952 | tf_op jit(solution)/shard_map/while/body/eval_jaxpr/reduce_sum | solution.py:21
  184.8 1.5 fusion.16
  186.3 1.1 bitcast_dynamic-update-slice_fusion.2
  187.5 9.0 %select_reduce_fusion.2 = f32[128,2432]{1,0:T(8,128)S(1)} fusion(f32[128,32]{1,0:T(8,128)S(1)} %dynamic-slice_bitcast_fusion.4, s32[128,32]{1,0:T(8,128)S(1)} %dynamic-slice_bitcast_fusion.5), kind=kLoop, calls=%fused_computation.2.clone.1 | loop fusion | flops 29573120 | bytes 1277952 | tf_op jit(solution)/shard_map/while/body/eval_jaxpr/reduce_sum | solution.py:21
  196.5 1.5 fusion.16
  198.0 1.2 bitcast_dynamic-update-slice_fusion.2
  199.2 9.0 %select_reduce_fusion.2 = f32[128,2432]{1,0:T(8,128)S(1)} fusion(f32[128,32]{1,0:T(8,128)S(1)} %dynamic-slice_bitcast_fusion.4, s32[128,32]{1,0:T(8,128)S(1)} %dynamic-slice_bitcast_fusion.5), kind=kLoop, calls=%fused_computation.2.clone.1 | loop fusion | flops 29573120 | bytes 1277952 | tf_op jit(solution)/shard_map/while/body/eval_jaxpr/reduce_sum | solution.py:21
  208.3 1.5 fusion.16
  209.8 1.2 bitcast_dynamic-update-slice_fusion.2
  211.0 67.4 %all-reduce = (f32[512]{0:T(512)S(1)}, f32[512]{0:T(512)S(1)}) all-reduce(f32[512]{0:T(512)S(1)} %exponential_reduce_fusion, f32[512]{0:T(512)S(1)} %bitcast.49), channel_id=1, replica_groups=mesh['dp'=8,'segment'=32] {'segment'}, use_global_device_ids=true, to_apply=%region_12.13 | all-reduce | flops 1024 | bytes 8192 | tf_op jit(solution)/shard_map/psum | solution.py:57
  278.4 0.0 copy-done.1
  278.4 1.2 fusion.10
  279.6 25.1 %all-reduce.1 = (f32[]{:T(128)}, f32[]{:T(128)}) all-reduce(f32[]{:T(128)} %get-tuple-element.67, f32[]{:T(128)} %get-tuple-element.66), channel_id=1, replica_groups=mesh['dp'=8,'segment'=32] {'dp'}, use_global_device_ids=true, to_apply=%region_14.15 | all-reduce | flops 2 | bytes 16 | tf_op jit(solution)/shard_map/psum | solution.py:61
  304.7 0.6 multiply_divide_fusion
  305.3 5.0 fusion.4
  310.3 9.6 %convolution_bitcast_fusion = f32[2048,512]{0,1:T(8,128)} fusion(bf16[512,2432]{1,0:T(8,128)(2,1)S(1)} %fusion.4, bf16[2048,2432]{1,0:T(8,128)(2,1)} %param.10), kind=kOutput, calls=%fused_computation.14 | convolution fusion | flops 5100273664 | bytes 16646144 | tf_op jit(solution)/shard_map/dot_general | solution.py:68
  319.9 0.0 copy-start
  319.9 5.4 copy.24
  325.3 0.0 reduce-scatter.4.cloned.1.call-update
  325.3 0.0 copy-done
  325.3 0.1 copy.22
  325.4 0.1 dynamic_slice.15
  326.9 147.4 %reduce-scatter.4.cloned.1.call-done = f32[64,512]{1,0:T(8,128)} async-done(((f32[2048,512]{1,0:T(8,128)}), f32[64,512]{1,0:T(8,128)}) %reduce-scatter.4.cloned.1.call-update) | async-done | bytes 131088
  474.3 1.0 copy.25
  475.3 0.2 fusion.8
  475.5 67.6 %psum.39 = f32[512]{0:T(512)S(1)} all-reduce(f32[512]{0:T(512)S(1)} %fusion.8), channel_id=1, replica_groups=mesh['dp'=8,'segment'=32] {'segment'}, use_global_device_ids=true, to_apply=%region_19.20 | all-reduce | flops 512 | bytes 4096 | tf_op jit(solution)/shard_map/psum | solution.py:76
  543.1 0.2 fusion.9
  543.3 0.8 copy.23
  (17 shorter events, 0.2 us)
Async XLA Ops:
  7.2 71.0 %copy-start.2 = (f32[2048]{0:T(1024)S(1)}, f32[2048]{0:T(1024)}, u32[]{:S(2)}) copy-start(f32[2048]{0:T(1024)} %param.9) | copy-start | bytes 24580
  7.2 68.5 %all-gather.2.cloned.1.call-start = ((), (), s32[]{:S(2)}) async-start(), calls=%async_computation.1 | async-start | bytes 4325376 | tf_op jit(solution)/shard_map/all_gather | solution.py:43
  7.9 466.4 %reduce-scatter.4.cloned.1.call-start = ((), (), s32[]{:S(2)}) async-start(), calls=%async_computation.2 | async-start | bytes 4325376
  163.9 114.4 %copy-start.1 = (f32[512]{0:T(512)S(1)}, f32[512]{0:T(512)}, u32[]{:S(2)}) copy-start(f32[512]{0:T(512)} %param.13) | copy-start | bytes 6148
  319.9 5.4 copy-start
Sparse Core Ops, SparseCore 0:
  9.9 65.7 all-gather.1
  325.4 148.8 reduce-scatter.3
where the time goes:
time: 553 us; the launch traced here: 552 us
  blocking collectives  231 us (42%)
  waiting for transfers between devices  212 us (38%)
  other arithmetic  58.5 us (11%)
  matrix products  21.6 us (4%)
  between operations  16.6 us (3%)
  local copies, waits for them, and re-layouts  12.5 us (2%)
    unnamed x3, waiting for transfers between devices  148 us
    pmax x1, blocking collectives, shards(): row_max = lax.pmax(local_max, 'segment')  70.5 us
    psum x1, blocking collectives, shards(): dot_total = lax.psum(jnp.sum(scaled * hidden_rows, axis=1), 'segment')  67.6 us
    psum x1, blocking collectives, shards(): exp_total, pick_total = lax.psum((local_sum, weighted_pick), 'segment')  67.4 us
    all_gather x1, waiting for transfers between devices, shards(): whole_rows = lax.all_gather(hidden_rows, 'segment', axis=1, tiled=True)  63.9 us
    reduce_sum x4, other arithmetic, one_block(): jnp.sum(jnp.where(matches, prob_block[:, :, None], 0.0), axis=1)  36.2 us
    psum x1, blocking collectives, shards(): lax.psum((jnp.sum(token_weights), local_loss), 'dp')  25.1 us
    dot_general x1, matrix products, shards(): logits = jnp.dot(normed, head_weight, preferred_element_type=jnp.float32)  12 us
  transfers between devices with their start and end apart: 2, of which 2 were waited for; matrix products, arithmetic and copies ran while one was open for 1% of the time, Pallas kernels for 0%

commit v1 on v0

v1 whole, which is shorter than its diff:
```python
import functools

import jax
import jax.numpy as jnp
from jax import lax
from jax.experimental import pallas as pl
from jax.experimental.pallas import tpu as pltpu
from jax.sharding import PartitionSpec as P

D = 2048
EPSILON = 1e-06
NZ, NX, NC = 4, 4, 2
LOG2E = 1.4426950408889634
NT = (((1,), (1,)), ((), ()))
MESH = pl.DeviceIdType.MESH
F32, BF16 = jnp.float32, jnp.bfloat16


def kernel(
    cfg,
    h_hbm, g_hbm, w_hbm, ids_hbm, tl_hbm, wt_hbm,
    loss_out, mean_out, grad_out,
    h, g, w, ids, tl, wt,
    gcol, hb, lhs, logit, targ, gl, hi_x, lo_x, p1_x, p2_x,
    icol, acol, stat, sq1, sq2, st1, st2, dps, ent, rows,
    gs, sib_s, sib_r, rl_s, rl_r, dr_s, dr_r, z_s, z_r,
    lossv, meanv, gradv,
    local_sem, gath_r, gath_s, sq_r, sq_s, st_r, st_s, dp_r, dp_s, rs_r, rs_s,
):
    NB, TB, VS, ndp, tokens = cfg
    T = NB * TB
    Q = TB // 128
    FD = D // (NZ * NX * NC)
    VT = VS // 128
    seg = lax.axis_index("segment")
    dpi = lax.axis_index("dp")
    c = lax.rem(seg, NC)
    x = lax.rem(lax.div(seg, NC), NX)
    z = lax.div(seg, NC * NX)
    oc = 1 - c
    sends = []

    def at(zz, xx, cc):
        return (zz * NX + xx) * NC + cc

    sib = at(z, x, oc)
    xs = [x, lax.rem(x + 1, NX), lax.rem(x + 3, NX), lax.rem(x + 2, NX)]

    def zxor(d):
        if d == 1:
            return z + 1 - 2 * lax.rem(z, 2)
        if d == 2:
            return lax.rem(z + 2, 4)
        return 3 - z

    def remote(src, dst, ss, rs, seg_to):
        return pltpu.make_async_remote_copy(
            src_ref=src, dst_ref=dst, send_sem=ss, recv_sem=rs,
            device_id={"segment": seg_to}, device_id_type=MESH,
        )

    def send(src, dst, ss, rs, seg_to):
        cp = remote(src, dst, ss, rs, seg_to)
        cp.start()
        sends.append(cp)

    def wait_recv(dst, ss, rs):
        remote(dst, dst, ss, rs, sib).wait_recv()

    loads = [
        pltpu.make_async_copy(a, b, local_sem.at[i])
        for i, (a, b) in enumerate(
            [(h_hbm, h), (g_hbm, g), (tl_hbm, tl), (ids_hbm, ids), (wt_hbm, wt)]
        )
    ]
    for cp in loads:
        cp.start()
    wloads = [
        pltpu.make_async_copy(w_hbm.at[:, xs[i]], w.at[:, xs[i]], local_sem.at[5 + i])
        for i in range(NX)
    ]
    for cp in wloads:
        cp.start()
    barrier = pltpu.get_barrier_semaphore()
    partners = []
    for i in range(NX):
        for j in range(NC):
            if i or j:
                partners.append({"segment": at(z, xs[i], lax.rem(c + j, NC))})
    for d in (1, 2, 3):
        partners.append({"segment": at(zxor(d), x, c)})
    for d in range(1, ndp):
        partners.append({"dp": lax.rem(dpi + d, ndp)})
    for p in partners:
        pl.semaphore_signal(barrier, inc=1, device_id=p, device_id_type=MESH)

    loads[0].wait()
    loads[1].wait()
    grow = g[pl.ds(z * NX + x, 1), :]
    gcol[...] = jnp.transpose(jnp.broadcast_to(grow, (128, 128)))
    gown = gcol[pl.ds(c * FD, FD), :]
    hv = h[...]
    hg = hv * jnp.concatenate([gown] * (T // 128), axis=1)
    for b in range(NB):
        hb[b, z, x, c] = hg[:, b * TB : (b + 1) * TB].astype(BF16)
    sqrow = jnp.sum(hv * hv, axis=0, keepdims=True)
    slot = x * NC + c
    sq1[slot] = jnp.zeros((8, 128), F32)
    for r in range(T // 128):
        sq1[slot, r : r + 1, :] = sqrow[:, r * 128 : (r + 1) * 128]
    pl.semaphore_wait(barrier, len(partners))

    gath_count = [0] * NB

    def g_send(b, zz, xx, cc, seg_to):
        n = gath_count[b]
        gath_count[b] += 1
        ref = hb.at[b, zz, xx, cc]
        send(ref, ref, gath_s.at[b, n], gath_r.at[b, at(zz, xx, cc)], seg_to)

    def g_wait(b, zz, xx, cc):
        wait_recv(hb.at[b, zz, xx, cc], gath_s.at[b, 0], gath_r.at[b, at(zz, xx, cc)])

    def g_own(b):
        g_send(b, z, x, c, at(z, xs[1], c))
        g_send(b, z, x, c, at(z, xs[2], c))
        for d in (1, 2, 3):
            g_send(b, z, x, c, at(zxor(d), x, c))
        g_send(b, z, x, c, sib)

    def g_z(b):
        for d in (1, 2, 3):
            zz = zxor(d)
            g_wait(b, zz, x, c)
            g_send(b, zz, x, c, at(z, xs[1], c))
            g_send(b, zz, x, c, at(z, xs[2], c))
            g_send(b, zz, x, c, sib)

    def g_x(b):
        for d in (0, 1, 2, 3):
            zz = z if d == 0 else zxor(d)
            g_wait(b, zz, xs[2], c)
            g_wait(b, zz, xs[1], c)
            high = lax.div(zz, 2)
            src_x = xs[2] + high * (xs[1] - xs[2])
            dst_x = xs[1] + high * (xs[2] - xs[1])
            g_send(b, zz, src_x, c, at(z, dst_x, c))
            g_send(b, zz, xs[2], c, sib)
            g_send(b, zz, xs[1], c, sib)

    def g_relay(b):
        for d in (0, 1, 2, 3):
            zz = z if d == 0 else zxor(d)
            g_wait(b, zz, xs[3], c)
            g_send(b, zz, xs[3], c, sib)

    def l_col(b, i):
        xx = xs[i]
        for d in (0, 1, 2, 3):
            zz = z if d == 0 else zxor(d)
            g_wait(b, zz, xx, oc)
        if b == 0:
            wloads[i].wait()
        blk = hb[b, :, xx].reshape(NZ * NC * FD, TB)
        lhs[...] = jnp.transpose(blk)
        step = 768
        full = VS // step

        def tile(n0, width):
            wt_ = w[:, xx, :, pl.ds(n0, width)].reshape(NZ * NC * FD, width)
            r = jnp.dot(lhs[...], wt_, preferred_element_type=F32)
            if i == 0:
                logit[b, :, pl.ds(n0, width)] = r
            else:
                logit[b, :, pl.ds(n0, width)] += r

        def body(n, carry):
            tile(pl.multiple_of(n * step, 128), step)
            return carry

        if full:
            lax.fori_loop(0, full, body, 0)
        if VS - full * step:
            tile(full * step, VS - full * step)

    def sq_first():
        n = 0
        for i in range(NX):
            for j in range(NC):
                if i or j:
                    ref = sq1.at[slot]
                    send(ref, ref, sq_s.at[n], sq_r.at[slot], at(z, xs[i], lax.rem(c + j, NC)))
                    n += 1

    def sq_second():
        for i in range(NX):
            for j in range(NC):
                if i or j:
                    s_ = xs[i] * NC + lax.rem(c + j, NC)
                    wait_recv(sq1.at[s_], sq_s.at[0], sq_r.at[s_])
        sq2[z] = jnp.sum(sq1[...], axis=0)
        for d in (1, 2, 3):
            ref = sq2.at[z]
            send(ref, ref, sq_s.at[6 + d], sq_r.at[8 + z], at(zxor(d), x, c))

    def to_cols(v, r, ref, row0):
        col = jnp.transpose(jnp.broadcast_to(v[r : r + 1, :], (128, 128)))
        ref[pl.ds(row0, 128), :] = col

    def sq_final():
        for d in (1, 2, 3):
            s_ = zxor(d)
            wait_recv(sq2.at[s_], sq_s.at[0], sq_r.at[8 + s_])
        inv = lax.rsqrt(jnp.sum(sq2[...], axis=0) / D + EPSILON)
        rows[0] = inv
        for r in range(T // 128):
            to_cols(inv, r, icol, r * 128)

    def teacher():
        loads[2].wait()
        loads[3].wait()
        t = tl[...]
        sh = t - jnp.max(t, axis=0, keepdims=True)
        logq = sh - jnp.log(jnp.sum(jnp.exp(sh), axis=0, keepdims=True))
        p = jnp.exp(logq)
        hrow = jnp.sum(p * logq, axis=0, keepdims=True)
        for r in range(T // 128):
            ent[r : r + 1, :] = hrow[:, r * 128 : (r + 1) * 128]
        local = ids[...] - seg * VS
        valid = (local >= 0) & (local < VS)
        hi = jnp.where(valid, lax.shift_right_logical(jnp.where(valid, local, 0), 7), -1)
        lo = jnp.where(valid, local, 0) & 127
        p1 = p.astype(BF16).astype(F32)
        p2 = p - p1
        allv = jnp.concatenate([hi.astype(F32), lo.astype(F32), p1, p2], axis=0)
        k = p.shape[0]
        cols = jnp.transpose(allv).astype(BF16)
        lane = lax.broadcasted_iota(jnp.int32, (4 * k, 8 * k), 1)
        row = lax.broadcasted_iota(jnp.int32, (4 * k, 8 * k), 0)
        lk = lane & (k - 1)
        tok = lax.broadcasted_iota(jnp.int32, (T, 8 * k), 0) & 7
        tl_lane = lax.shift_right_logical(
            lax.broadcasted_iota(jnp.int32, (T, 8 * k), 1), 5
        )
        own = tok == tl_lane
        for j, ref in enumerate((hi_x, lo_x, p1_x, p2_x)):
            pick = jnp.where(row == lk + j * k, 1.0, 0.0).astype(BF16)
            v = jnp.dot(cols, pick, preferred_element_type=F32)
            ref[...] = v if j == 0 else jnp.where(own, v, 0.0)

    def targets(b, lo_blk, hi_blk):
        sub = lax.broadcasted_iota(jnp.int32, (128, 256), 0).astype(F32)

        def body(n, carry):
            r0 = pl.multiple_of(b * TB + n * 8, 8)
            hx = hi_x[pl.ds(r0, 8), :]
            a1 = p1_x[pl.ds(r0, 8), :]
            a2 = p2_x[pl.ds(r0, 8), :]
            lrow = jnp.sum(lo_x[pl.ds(r0, 8), :], axis=0, keepdims=True)
            bt = jnp.where(sub == lrow, 1.0, 0.0).astype(BF16)
            masks = [hx == float(j) for j in range(VT)]
            a = jnp.concatenate(
                [jnp.where(m, a1, 0.0) for m in masks]
                + [jnp.where(m, a2, 0.0) for m in masks],
                axis=0,
            ).astype(BF16)
            o = lax.dot_general(a, bt, NT, preferred_element_type=F32)
            o = o[: 8 * VT] + o[8 * VT :]
            for j in range(VT):
                targ[b, pl.ds(pl.multiple_of(n * 8, 8), 8), j * 128 : (j + 1) * 128] = (
                    o[j * 8 : (j + 1) * 8]
                )
            return carry

        lax.fori_loop(lo_blk, hi_blk, body, 0, unroll=2)

    def softmax(b):
        lane = lax.broadcasted_iota(jnp.int32, (8, 128), 1)

        def body(n, carry):
            r0 = pl.multiple_of(n * 8, 8)
            raw = [logit[b, pl.ds(r0, 8), j * 128 : (j + 1) * 128] for j in range(VT)]
            mx = functools.reduce(jnp.maximum, raw)
            mx = jnp.max(mx, axis=1, keepdims=True)
            iv = icol[pl.ds(pl.multiple_of(b * TB + n * 8, 8), 8), :]
            sc = iv * LOG2E
            m = jnp.broadcast_to(mx, (8, 128))
            s = jnp.zeros((8, 128), F32)
            sl = jnp.zeros((8, 128), F32)
            pk = jnp.zeros((8, 128), F32)
            for j in range(VT):
                e = jnp.exp2((raw[j] - m) * sc)
                logit[b, pl.ds(r0, 8), j * 128 : (j + 1) * 128] = e
                s += e
                sl += e * raw[j]
                pk += targ[b, pl.ds(r0, 8), j * 128 : (j + 1) * 128] * raw[j]
            s = jnp.sum(s, axis=1, keepdims=True)
            sl = jnp.sum(sl, axis=1, keepdims=True)
            pk = jnp.sum(pk, axis=1, keepdims=True)
            stat[pl.ds(r0, 8), :] = jnp.where(
                lane == 0, m * iv, jnp.where(lane == 1, s, jnp.where(lane == 2, sl, pk))
            )
            return carry

        lax.fori_loop(0, TB // 8, body, 0, unroll=2)
        for q in range(Q):
            tr = jnp.transpose(stat[q * 128 : (q + 1) * 128, :])
            for k in range(4):
                st1[b, slot, k * Q + q : k * Q + q + 1, :] = tr[k : k + 1, :]
        n = 0
        for i in range(NX):
            for j in range(NC):
                if i or j:
                    ref = st1.at[b, slot]
                    send(ref, ref, st_s.at[b, n], st_r.at[b, slot],
                         at(z, xs[i], lax.rem(c + j, NC)))
                    n += 1

    def merge(ref, b):
        m = ref[b, :, 0:Q, :]
        top = jnp.max(m, axis=0)
        wgt = jnp.exp(m - top[None])
        s = jnp.sum(wgt * ref[b, :, Q : 2 * Q, :], axis=0)
        sl = jnp.sum(wgt * ref[b, :, 2 * Q : 3 * Q, :], axis=0)
        pk = jnp.sum(ref[b, :, 3 * Q : 4 * Q, :], axis=0)
        return top, s, sl, pk

    def stat_second(b):
        for i in range(NX):
            for j in range(NC):
                if i or j:
                    s_ = xs[i] * NC + lax.rem(c + j, NC)
                    wait_recv(st1.at[b, s_], st_s.at[b, 0], st_r.at[b, s_])
        for k, v in enumerate(merge(st1, b)):
            st2[b, z, k * Q : (k + 1) * Q, :] = v
        for d in (1, 2, 3):
            ref = st2.at[b, z]
            send(ref, ref, st_s.at[b, 6 + d], st_r.at[b, 8 + z], at(zxor(d), x, c))

    def stat_final(b):
        for d in (1, 2, 3):
            s_ = zxor(d)
            wait_recv(st2.at[b, s_], st_s.at[b, 0], st_r.at[b, 8 + s_])
        top, s, sl, pk = merge(st2, b)
        total = top + jnp.log(s)
        inv = rows[0, b * Q : (b + 1) * Q, :]
        lossv[b * Q : (b + 1) * Q, :] = ent[b * Q : (b + 1) * Q, :] - inv * pk + total
        rows[1, b * Q : (b + 1) * Q, :] = sl / s - pk
        scale = jnp.exp(st1[b, slot, 0:Q, :] - total)
        for q in range(Q):
            to_cols(scale, q, acol, q * 128)

    def make_gl(b):
        def body(n, carry):
            r0 = pl.multiple_of(n * 16, 16)
            a = acol[pl.ds(r0, 16), :]
            for j in range(VT):
                sl_ = slice(j * 128, (j + 1) * 128)
                gl[pl.ds(r0, 16), sl_] = (
                    logit[b, pl.ds(r0, 16), sl_] * a - targ[b, pl.ds(r0, 16), sl_]
                ).astype(BF16)
            return carry

        lax.fori_loop(0, TB // 16, body, 0)

    order = [3, 1, 2, 0]

    def mm(b, k):
        xx = xs[order[k]]
        wt_ = w[:, xx].reshape(NZ * NC * FD, VS)
        r = lax.dot_general(wt_, gl[...], NT, preferred_element_type=F32)
        gs[k] = r.reshape(NZ, NC, FD, TB)
        sib_s[b, k] = gs[k, :, oc].astype(BF16)
        send(sib_s.at[b, k], sib_r.at[b, k], rs_s.at[b, k], rs_r.at[b, k], sib)

    def pair(b, k):
        wait_recv(sib_r.at[b, k], rs_s.at[b, 0], rs_r.at[b, k])
        return gs[k, :, c] + sib_r[b, k].astype(F32)

    def rs_col(b, k):
        v = pair(b, k)
        if k == 0:
            rl_s[b] = v.astype(BF16).reshape(2, 2, FD, TB)
            send(rl_s.at[b, 0], rl_r.at[b, 0], rs_s.at[b, 4], rs_r.at[b, 4], at(z, xs[1], c))
            send(rl_s.at[b, 1], rl_r.at[b, 1], rs_s.at[b, 5], rs_r.at[b, 5], at(z, xs[2], c))
        elif k in (1, 2):
            j = k - 1
            wait_recv(rl_r.at[b, j], rs_s.at[b, 0], rs_r.at[b, 4 + j])
            v = v.reshape(2, 2, FD, TB)
            dr_s[b, j, j] = (v[j] + rl_r[b, j].astype(F32)).astype(BF16)
            dr_s[b, j, 1 - j] = v[1 - j].astype(BF16)
            send(dr_s.at[b, j], dr_r.at[b, j], rs_s.at[b, 6 + j], rs_r.at[b, 6 + j],
                 at(z, xs[k], c))
        else:
            for j in (0, 1):
                wait_recv(dr_r.at[b, j], rs_s.at[b, 0], rs_r.at[b, 6 + j])
            v = v.reshape(2, 2, FD, TB) + dr_r[b, 0].astype(F32) + dr_r[b, 1].astype(F32)
            gs[3, :, 0] = v.reshape(NZ, FD, TB)
            z_s[b] = v.reshape(NZ, FD, TB).astype(BF16)
            for d in (1, 2, 3):
                zz = zxor(d)
                send(z_s.at[b, zz], z_r.at[b, z], rs_s.at[b, 7 + d], rs_r.at[b, 8 + z],
                     at(zz, x, c))
            gradv[:, b * TB : (b + 1) * TB] = gs[3, z, 0]

    def row_of(v, b):
        return jnp.concatenate([v[b * Q + q : b * Q + q + 1, :] for q in range(Q)], axis=1)

    def finish(b):
        cols = slice(b * TB, (b + 1) * TB)
        tot = gradv[:, cols]
        for d in (1, 2, 3):
            s_ = zxor(d)
            wait_recv(z_r.at[b, s_], rs_s.at[b, 0], rs_r.at[b, 8 + s_])
            tot = tot + z_r[b, s_].astype(F32)
        inv = rows[0]
        first = row_of(inv * rows[2], b)
        second = row_of(inv * inv * rows[1] / D, b)
        gn = jnp.concatenate([gcol[pl.ds(c * FD, FD), :]] * Q, axis=1)
        gradv[:, cols] = first * (gn * tot - h[:, cols] * second)

    def dp_send():
        wv = wt[...]
        lane_sum = lambda v: jnp.sum(jnp.sum(v, axis=1, keepdims=True), axis=0, keepdims=True)
        dps[dpi] = jnp.zeros((8, 128), F32)
        dps[dpi, 0:1, :] = jnp.broadcast_to(lane_sum(wv), (1, 128))
        dps[dpi, 1:2, :] = jnp.broadcast_to(lane_sum(wv * lossv[...]), (1, 128))
        for d in range(1, ndp):
            cp = pltpu.make_async_remote_copy(
                src_ref=dps.at[dpi], dst_ref=dps.at[dpi], send_sem=dp_s.at[d],
                recv_sem=dp_r.at[dpi], device_id={"dp": lax.rem(dpi + d, ndp)},
                device_id_type=MESH,
            )
            cp.start()
            sends.append(cp)

    def dp_final():
        for d in range(1, ndp):
            s_ = lax.rem(dpi + d, ndp)
            wait_recv(dps.at[s_], dp_s.at[0], dp_r.at[s_])
        tot = jnp.sum(dps[...], axis=0)
        meanv[...] = jnp.broadcast_to(tot[1:2, :] / tot[0:1, :], meanv.shape)
        rows[2, 0 : T // 128, :] = wt[...] * tokens / tot[0:1, :]

    nblk = TB // 8
    if NB == 1:
        g_own(0)
        sq_first()
        teacher()
        targets(0, 0, nblk // 4)
        g_z(0)
        sq_second()
        targets(0, nblk // 4, nblk // 2)
        l_col(0, 0)
        g_x(0)
        targets(0, nblk // 2, nblk)
        l_col(0, 1)
        g_relay(0)
        l_col(0, 2)
        sq_final()
        l_col(0, 3)
        softmax(0)
        loads[4].wait()
        stat_second(0)
        stat_final(0)
        dp_send()
        make_gl(0)
        mm(0, 0)
        mm(0, 1)
        rs_col(0, 0)
        mm(0, 2)
        rs_col(0, 1)
        mm(0, 3)
        rs_col(0, 2)
        dp_final()
        rs_col(0, 3)
        finish(0)
    else:
        g_own(0)
        sq_first()
        teacher()
        targets(0, 0, nblk // 2)
        g_z(0)
        g_own(1)
        sq_second()
        targets(0, nblk // 2, nblk)
        l_col(0, 0)
        g_x(0)
        g_z(1)
        l_col(0, 1)
        g_relay(0)
        l_col(0, 2)
        sq_final()
        g_x(1)
        l_col(0, 3)
        softmax(0)
        targets(1, 0, nblk)
        g_relay(1)
        l_col(1, 0)
        stat_second(0)
        l_col(1, 1)
        stat_final(0)
        make_gl(0)
        mm(0, 0)
        l_col(1, 2)
        rs_col(0, 0)
        l_col(1, 3)
        softmax(1)
        mm(0, 1)
        rs_col(0, 1)
        mm(0, 2)
        rs_col(0, 2)
        stat_second(1)
        mm(0, 3)
        stat_final(1)
        loads[4].wait()
        dp_send()
        rs_col(0, 3)
        make_gl(1)
        mm(1, 0)
        mm(1, 1)
        rs_col(1, 0)
        mm(1, 2)
        rs_col(1, 1)
        dp_final()
        finish(0)
        mm(1, 3)
        rs_col(1, 2)
        rs_col(1, 3)
        finish(1)

    outs = [
        pltpu.make_async_copy(a, b, local_sem.at[9 + i])
        for i, (a, b) in enumerate([(lossv, loss_out), (meanv, mean_out), (gradv, grad_out)])
    ]
    for cp in outs:
        cp.start()
    for cp in sends:
        cp.wait_send()
    for cp in outs:
        cp.wait()


NB_TOKENS = 2


def shards(hidden_rows, norm_gain, head_weight, teacher_ids, teacher_logits, token_weights):
    T, FD = hidden_rows.shape
    VS = head_weight.shape[1]
    K = teacher_ids.shape[1]
    ndp = lax.axis_size("dp")
    NB = NB_TOKENS
    TB = T // NB
    Q = TB // 128
    any_ = pl.BlockSpec(memory_space=pl.ANY)
    V = pltpu.VMEM
    dma = pltpu.SemaphoreType.DMA
    scratch = [
        V((FD, T), F32), V((NZ * NX, 128), F32), V((NZ, NX, NC * FD, VS), BF16),
        V((K, T), jnp.int32), V((K, T), F32), V((T // 128, 128), F32),
        V((128, 128), F32),
        V((NB, NZ, NX, NC, FD, TB), BF16),
        V((TB, NZ * NC * FD), BF16),
        V((NB, TB, VS), F32),
        V((NB, TB, VS), F32),
        V((TB, VS), BF16),
        V((T, 8 * K), F32), V((T, 8 * K), F32), V((T, 8 * K), F32), V((T, 8 * K), F32),
        V((T, 128), F32), V((TB, 128), F32), V((TB, 128), F32),
        V((NX * NC, 8, 128), F32), V((NZ, 8, 128), F32),
        V((NB, NX * NC, 4 * Q, 128), F32), V((NB, NZ, 4 * Q, 128), F32),
        V((ndp, 8, 128), F32), V((T // 128, 128), F32), V((3, 8, 128), F32),
        V((4, NZ, NC, FD, TB), F32),
        V((NB, 4, NZ, FD, TB), BF16), V((NB, 4, NZ, FD, TB), BF16),
        V((NB, 2, 2, FD, TB), BF16), V((NB, 2, 2, FD, TB), BF16),
        V((NB, 2, 2, 2, FD, TB), BF16), V((NB, 2, 2, 2, FD, TB), BF16),
        V((NB, NZ, FD, TB), BF16), V((NB, NZ, FD, TB), BF16),
        V((T // 128, 128), F32), V((8, 128), F32), V((FD, T), F32),
        dma((12,)), dma((NB, 32)), dma((NB, 31)), dma((12,)), dma((10,)),
        dma((NB, 12)), dma((NB, 10)), dma((ndp,)), dma((ndp,)), dma((NB, 12)), dma((NB, 11)),
    ]
    loss, mean, grad = pl.pallas_call(
        functools.partial(kernel, (NB, TB, VS, ndp, T * ndp)),
        out_shape=(
            jax.ShapeDtypeStruct((T // 128, 128), F32),
            jax.ShapeDtypeStruct((8, 128), F32),
            jax.ShapeDtypeStruct((FD, T), F32),
        ),
        in_specs=[any_] * 6,
        out_specs=(any_, any_, any_),
        scratch_shapes=scratch,
        compiler_params=pltpu.CompilerParams(
            collective_id=0, has_side_effects=True, vmem_limit_bytes=60 * 1024 * 1024
        ),
    )(
        hidden_rows.T,
        norm_gain.reshape(NZ * NX, 128),
        head_weight.reshape(NZ, NX, NC * FD, VS),
        teacher_ids.T,
        teacher_logits.T,
        token_weights.reshape(T // 128, 128),
    )
    return (loss.reshape(T), mean[0, 0], grad.T)


def solution(mesh):
    in_specs = (P("dp", "segment"), P(), P(None, "segment"), P("dp", None), P("dp", None), P("dp"))
    out_specs = (P("dp"), P(), P("dp", "segment"))
    return jax.shard_map(shards, mesh=mesh, in_specs=in_specs, out_specs=out_specs, check_vma=False)
```

time: 553 us -> 85.7 us (0.15)
  the two profiles are of different devices: /device:TPU:8 before, /device:TPU:6 now
where the time goes in v1:
time: 85.7 us; the launch traced here: 85.6 us
  Pallas kernels  80.9 us (94%)
  local copies, waits for them, and re-layouts  3.99 us (5%)
    pallas_call x1, Pallas kernels, shards(): pl.pallas_call(functools.partial(kernel, (NB, TB, VS, ndp, T * ndp)), out...  80.9 us
    unnamed x2, local copies, waits for them, and re-layouts  2.8 us

profile of v1, /device:TPU:6, one launch (start us, length us, event | category | flops | bytes accessed | tf_op | source)
XLA Modules:
  0.0 85.6 jit_solution(12141426657953081222)
XLA Ops:
  0.6 80.9 %shard_map.85 = (f32[4,128]{1,0:T(4,128)}, f32[8,128]{1,0:T(8,128)}, f32[64,512]{1,0:T(8,128)}) custom-call(f32[64,512]{1,0:T(8,128)} %bitcast.10, f32[16,128]{1,0:T(8,128)} %bitcast.14, bf16[4,4,128,2432]{3,2,1,0:T(8,128)(2,1)} %bitcast.9, s32[32,512]{1,0:T(8,128)} %bitcast.12, f32[32,512]{1,0:T(8,128)} %bitcast.13, f32[4,128]{1,0:T(4,128)} %bitcast.15), custom_call_target="tpu_custom_call" | custom-call | tf_op jit(solution)/shard_map/pallas_call | solution.py:581
  81.6 1.2 %slice.3 = f32[1,1]{1,0:T(1,128)} slice(f32[8,128]{1,0:T(8,128)} %get-tuple-element.7), slice={[0:1], [0:1]} | slice | bytes 8 | tf_op jit(solution)/shard_map/slice | solution.py:602
  82.8 1.2 %copy.11 = f32[512]{0:T(512)} copy(f32[512]{0:T(512)} %bitcast.16) | data formatting | bytes 4096
  84.0 1.6 %copy.12 = f32[512,64]{0,1:T(8,128)} copy(f32[512,64]{0,1:T(8,128)} %bitcast.11) | data formatting | bytes 262144

commit v2 on v1

--- a/solution.py
+++ b/solution.py
@@ -124,34 +124,42 @@
     def g_own(b):
         g_send(b, z, x, c, at(z, xs[1], c))
         g_send(b, z, x, c, at(z, xs[2], c))
-        for d in (1, 2, 3):
+        for d in (1, 3, 2):
             g_send(b, z, x, c, at(zxor(d), x, c))
         g_send(b, z, x, c, sib)
 
-    def g_z(b):
-        for d in (1, 2, 3):
+    def g_z(b, steps=(1, 3, 2)):
+        for d in steps:
             zz = zxor(d)
             g_wait(b, zz, x, c)
             g_send(b, zz, x, c, at(z, xs[1], c))
             g_send(b, zz, x, c, at(z, xs[2], c))
             g_send(b, zz, x, c, sib)
 
+    HR = FD // 2
+
+    def g_half(b, zz, xx, j):
+        return hb.at[b, zz, xx, c, pl.ds(j * HR, HR)]
+
+    def g_half_sem(b, zz, xx, j):
+        return gath_r.at[b, at(zz, xx, c) if j == 0 else 32 + zz]
+
     def g_x(b):
-        for d in (0, 1, 2, 3):
+        for d in (0, 1, 3, 2):
             zz = z if d == 0 else zxor(d)
-            g_wait(b, zz, xs[2], c)
-            g_wait(b, zz, xs[1], c)
-            high = lax.div(zz, 2)
-            src_x = xs[2] + high * (xs[1] - xs[2])
-            dst_x = xs[1] + high * (xs[2] - xs[1])
-            g_send(b, zz, src_x, c, at(z, dst_x, c))
-            g_send(b, zz, xs[2], c, sib)
-            g_send(b, zz, xs[1], c, sib)
+            for j, (src, dst) in enumerate(((xs[2], xs[1]), (xs[1], xs[2]))):
+                g_wait(b, zz, src, c)
+                n = gath_count[b]
+                gath_count[b] += 1
+                ref = g_half(b, zz, src, j)
+                send(ref, ref, gath_s.at[b, n], g_half_sem(b, zz, src, j), at(z, dst, c))
+                g_send(b, zz, src, c, sib)
 
     def g_relay(b):
-        for d in (0, 1, 2, 3):
+        for d in (0, 1, 3, 2):
             zz = z if d == 0 else zxor(d)
-            g_wait(b, zz, xs[3], c)
+            for j in (0, 1):
+                wait_recv(g_half(b, zz, xs[3], j), gath_s.at[b, 0], g_half_sem(b, zz, xs[3], j))
             g_send(b, zz, xs[3], c, sib)
 
     def l_col(b, i):
@@ -163,25 +171,16 @@
             wloads[i].wait()
         blk = hb[b, :, xx].reshape(NZ * NC * FD, TB)
         lhs[...] = jnp.transpose(blk)
-        step = 768
-        full = VS // step
-
-        def tile(n0, width):
-            wt_ = w[:, xx, :, pl.ds(n0, width)].reshape(NZ * NC * FD, width)
-            r = jnp.dot(lhs[...], wt_, preferred_element_type=F32)
-            if i == 0:
-                logit[b, :, pl.ds(n0, width)] = r
-            else:
-                logit[b, :, pl.ds(n0, width)] += r
-
-        def body(n, carry):
-            tile(pl.multiple_of(n * step, 128), step)
-            return carry
-
-        if full:
-            lax.fori_loop(0, full, body, 0)
-        if VS - full * step:
-            tile(full * step, VS - full * step)
+        wt_ = w[:, xx].reshape(NZ * NC * FD, VS)
+        r = jnp.dot(lhs[...], wt_, preferred_element_type=F32)
+        if i == 0:
+            logit[b] = r
+            return
+        r = r + logit[b]
+        logit[b] = r
+        if i == NX - 1:
+            tops = [r[:, j * 128 : (j + 1) * 128] for j in range(VT)]
+            stat[3] = functools.reduce(jnp.maximum, tops)
 
     def sq_first():
         n = 0
@@ -249,64 +248,72 @@
             ref[...] = v if j == 0 else jnp.where(own, v, 0.0)
 
     def targets(b, lo_blk, hi_blk):
-        sub = lax.broadcasted_iota(jnp.int32, (128, 256), 0).astype(F32)
+        sub = lax.broadcasted_iota(jnp.int32, (128, 256), 0).astype(F32).astype(BF16)
+        half = (lax.broadcasted_iota(jnp.int32, (16, 256), 0) // 8).astype(F32).astype(BF16)
+        nh = (VT + 1) // 2
+        one, zero = jnp.ones((), BF16), jnp.zeros((), BF16)
+
+        def twice(v):
+            return jnp.concatenate([v, v], axis=0).astype(BF16)
 
         def body(n, carry):
             r0 = pl.multiple_of(b * TB + n * 8, 8)
-            hx = hi_x[pl.ds(r0, 8), :]
-            a1 = p1_x[pl.ds(r0, 8), :]
-            a2 = p2_x[pl.ds(r0, 8), :]
-            lrow = jnp.sum(lo_x[pl.ds(r0, 8), :], axis=0, keepdims=True)
-            bt = jnp.where(sub == lrow, 1.0, 0.0).astype(BF16)
-            masks = [hx == float(j) for j in range(VT)]
+            hx = twice(hi_x[pl.ds(r0, 8), :]) - half
+            a1 = twice(p1_x[pl.ds(r0, 8), :])
+            a2 = twice(p2_x[pl.ds(r0, 8), :])
+            lrow = jnp.sum(lo_x[pl.ds(r0, 8), :], axis=0, keepdims=True).astype(BF16)
+            bt = jnp.where(sub == lrow, one, zero)
+            masks = [hx == jnp.asarray(2.0 * j, BF16) for j in range(nh)]
             a = jnp.concatenate(
-                [jnp.where(m, a1, 0.0) for m in masks]
-                + [jnp.where(m, a2, 0.0) for m in masks],
+                [jnp.where(m, a1, zero) for m in masks]
+                + [jnp.where(m, a2, zero) for m in masks],
                 axis=0,
-            ).astype(BF16)
+            )
             o = lax.dot_general(a, bt, NT, preferred_element_type=F32)
-            o = o[: 8 * VT] + o[8 * VT :]
+            o = o[: 16 * nh] + o[16 * nh :]
             for j in range(VT):
                 targ[b, pl.ds(pl.multiple_of(n * 8, 8), 8), j * 128 : (j + 1) * 128] = (
                     o[j * 8 : (j + 1) * 8]
                 )
             return carry
 
-        lax.fori_loop(lo_blk, hi_blk, body, 0, unroll=2)
+        lax.fori_loop(lo_blk, hi_blk, body, 0, unroll=4)
 
     def softmax(b):
-        lane = lax.broadcasted_iota(jnp.int32, (8, 128), 1)
+        R = 32
+        tops = stat[3]
+        for q in range(Q):
+            tr = jnp.transpose(tops[q * 128 : (q + 1) * 128])
+            mrow = jnp.max(tr, axis=0, keepdims=True)
+            r = b * Q + q
+            st1[b, slot, q : q + 1, :] = mrow * rows[0, r : r + 1, :]
+        stat[3] = jnp.broadcast_to(jnp.max(tops, axis=1, keepdims=True), (TB, 128))
 
         def body(n, carry):
-            r0 = pl.multiple_of(n * 8, 8)
-            raw = [logit[b, pl.ds(r0, 8), j * 128 : (j + 1) * 128] for j in range(VT)]
-            mx = functools.reduce(jnp.maximum, raw)
-            mx = jnp.max(mx, axis=1, keepdims=True)
-            iv = icol[pl.ds(pl.multiple_of(b * TB + n * 8, 8), 8), :]
-            sc = iv * LOG2E
-            m = jnp.broadcast_to(mx, (8, 128))
-            s = jnp.zeros((8, 128), F32)
-            sl = jnp.zeros((8, 128), F32)
-            pk = jnp.zeros((8, 128), F32)
+            r0 = pl.multiple_of(n * R, R)
+            sc = icol[pl.ds(pl.multiple_of(b * TB + n * R, R), R), :] * LOG2E
+            m = stat[3, pl.ds(r0, R), :]
+            s = jnp.zeros((R, 128), F32)
+            sl = jnp.zeros((R, 128), F32)
+            pk = jnp.zeros((R, 128), F32)
             for j in range(VT):
-                e = jnp.exp2((raw[j] - m) * sc)
-                logit[b, pl.ds(r0, 8), j * 128 : (j + 1) * 128] = e
+                raw = logit[b, pl.ds(r0, R), j * 128 : (j + 1) * 128]
+                e = jnp.exp2((raw - m) * sc)
+                logit[b, pl.ds(r0, R), j * 128 : (j + 1) * 128] = e
                 s += e
-                sl += e * raw[j]
-                pk += targ[b, pl.ds(r0, 8), j * 128 : (j + 1) * 128] * raw[j]
-            s = jnp.sum(s, axis=1, keepdims=True)
-            sl = jnp.sum(sl, axis=1, keepdims=True)
-            pk = jnp.sum(pk, axis=1, keepdims=True)
-            stat[pl.ds(r0, 8), :] = jnp.where(
-                lane == 0, m * iv, jnp.where(lane == 1, s, jnp.where(lane == 2, sl, pk))
-            )
+                sl += e * raw
+                pk += targ[b, pl.ds(r0, R), j * 128 : (j + 1) * 128] * raw
+            stat[0, pl.ds(r0, R), :] = s
+            stat[1, pl.ds(r0, R), :] = sl
+            stat[2, pl.ds(r0, R), :] = pk
             return carry
 
-        lax.fori_loop(0, TB // 8, body, 0, unroll=2)
+        lax.fori_loop(0, TB // R, body, 0, unroll=2)
         for q in range(Q):
-            tr = jnp.transpose(stat[q * 128 : (q + 1) * 128, :])
-            for k in range(4):
-                st1[b, slot, k * Q + q : k * Q + q + 1, :] = tr[k : k + 1, :]
+            for k in range(3):
+                tr = jnp.transpose(stat[k, q * 128 : (q + 1) * 128, :])
+                r = (k + 1) * Q + q
+                st1[b, slot, r : r + 1, :] = jnp.sum(tr, axis=0, keepdims=True)
         n = 0
         for i in range(NX):
             for j in range(NC):
@@ -369,39 +376,53 @@
         xx = xs[order[k]]
         wt_ = w[:, xx].reshape(NZ * NC * FD, VS)
         r = lax.dot_general(wt_, gl[...], NT, preferred_element_type=F32)
-        gs[k] = r.reshape(NZ, NC, FD, TB)
-        sib_s[b, k] = gs[k, :, oc].astype(BF16)
+        gs[b, k] = r.reshape(NZ, NC, FD, TB)
+        sib_s[b, k] = gs[b, k, :, oc].astype(BF16)
         send(sib_s.at[b, k], sib_r.at[b, k], rs_s.at[b, k], rs_r.at[b, k], sib)
 
     def pair(b, k):
         wait_recv(sib_r.at[b, k], rs_s.at[b, 0], rs_r.at[b, k])
-        return gs[k, :, c] + sib_r[b, k].astype(F32)
+        return gs[b, k, :, c] + sib_r[b, k].astype(F32)
 
     def rs_col(b, k):
         v = pair(b, k)
         if k == 0:
-            rl_s[b] = v.astype(BF16).reshape(2, 2, FD, TB)
-            send(rl_s.at[b, 0], rl_r.at[b, 0], rs_s.at[b, 4], rs_r.at[b, 4], at(z, xs[1], c))
-            send(rl_s.at[b, 1], rl_r.at[b, 1], rs_s.at[b, 5], rs_r.at[b, 5], at(z, xs[2], c))
-        elif k in (1, 2):
+            for j in (0, 1):
+                rl_s[b, j] = v[:, j * HR : (j + 1) * HR].astype(BF16)
+            for d in (1, 3, 2, 0):
+                zz = z if d == 0 else zxor(d)
+                for j in (0, 1):
+                    n = 4 + 4 * j + zz
+                    send(rl_s.at[b, j, zz], rl_r.at[b, j, zz], rs_s.at[b, n], rs_r.at[b, n],
+                         at(z, xs[1 + j], c))
+            return
+        gs[b, k, :, 0] = v
+        if k in (1, 2):
             j = k - 1
-            wait_recv(rl_r.at[b, j], rs_s.at[b, 0], rs_r.at[b, 4 + j])
-            v = v.reshape(2, 2, FD, TB)
-            dr_s[b, j, j] = (v[j] + rl_r[b, j].astype(F32)).astype(BF16)
-            dr_s[b, j, 1 - j] = v[1 - j].astype(BF16)
-            send(dr_s.at[b, j], dr_r.at[b, j], rs_s.at[b, 6 + j], rs_r.at[b, 6 + j],
-                 at(z, xs[k], c))
-        else:
+            for d in (1, 3, 2, 0):
+                zz = z if d == 0 else zxor(d)
+                wait_recv(rl_r.at[b, j, zz], rs_s.at[b, 0], rs_r.at[b, 4 + 4 * j + zz])
+                u = gs[b, k, zz, 0]
+                part = u[j * HR : (j + 1) * HR] + rl_r[b, j, zz].astype(F32)
+                rest = u[(1 - j) * HR : (2 - j) * HR]
+                dr_s[b, j, zz] = jnp.concatenate(
+                    [part, rest] if j == 0 else [rest, part], axis=0
+                ).astype(BF16)
+                n = 12 + 4 * j + zz
+                send(dr_s.at[b, j, zz], dr_r.at[b, j, zz], rs_s.at[b, n], rs_r.at[b, n],
+                     at(z, xs[k], c))
+            return
+        for d in (1, 3, 2, 0):
+            zz = z if d == 0 else zxor(d)
             for j in (0, 1):
-                wait_recv(dr_r.at[b, j], rs_s.at[b, 0], rs_r.at[b, 6 + j])
-            v = v.reshape(2, 2, FD, TB) + dr_r[b, 0].astype(F32) + dr_r[b, 1].astype(F32)
-            gs[3, :, 0] = v.reshape(NZ, FD, TB)
-            z_s[b] = v.reshape(NZ, FD, TB).astype(BF16)
-            for d in (1, 2, 3):
-                zz = zxor(d)
-                send(z_s.at[b, zz], z_r.at[b, z], rs_s.at[b, 7 + d], rs_r.at[b, 8 + z],
+                wait_recv(dr_r.at[b, j, zz], rs_s.at[b, 0], rs_r.at[b, 12 + 4 * j + zz])
+            u = gs[b, 3, zz, 0] + dr_r[b, 0, zz].astype(F32) + dr_r[b, 1, zz].astype(F32)
+            if d:
+                z_s[b, zz] = u.astype(BF16)
+                send(z_s.at[b, zz], z_r.at[b, z], rs_s.at[b, 19 + d], rs_r.at[b, 20 + z],
                      at(zz, x, c))
-            gradv[:, b * TB : (b + 1) * TB] = gs[3, z, 0]
+            else:
+                gradv[:, b * TB : (b + 1) * TB] = u
 
     def row_of(v, b):
         return jnp.concatenate([v[b * Q + q : b * Q + q + 1, :] for q in range(Q)], axis=1)
@@ -411,7 +432,7 @@
         tot = gradv[:, cols]
         for d in (1, 2, 3):
             s_ = zxor(d)
-            wait_recv(z_r.at[b, s_], rs_s.at[b, 0], rs_r.at[b, 8 + s_])
+            wait_recv(z_r.at[b, s_], rs_s.at[b, 0], rs_r.at[b, 20 + s_])
             tot = tot + z_r[b, s_].astype(F32)
         inv = rows[0]
         first = row_of(inv * rows[2], b)
@@ -478,54 +499,56 @@
     else:
         g_own(0)
         sq_first()
+        g_own(1)
         teacher()
-        targets(0, 0, nblk // 2)
-        g_z(0)
-        g_own(1)
+        targets(0, 0, nblk // 4)
+        g_z(0, (1,))
+        targets(0, nblk // 4, nblk)
+        g_z(0, (3, 2))
         sq_second()
-        targets(0, nblk // 2, nblk)
+        targets(1, 0, nblk // 2)
+        g_x(0)
         l_col(0, 0)
-        g_x(0)
         g_z(1)
+        targets(1, nblk // 2, nblk)
+        g_relay(0)
         l_col(0, 1)
-        g_relay(0)
         l_col(0, 2)
+        g_x(1)
         sq_final()
-        g_x(1)
         l_col(0, 3)
         softmax(0)
-        targets(1, 0, nblk)
+        l_col(1, 0)
         g_relay(1)
-        l_col(1, 0)
+        l_col(1, 1)
+        l_col(1, 2)
         stat_second(0)
-        l_col(1, 1)
+        l_col(1, 3)
+        softmax(1)
         stat_final(0)
         make_gl(0)
         mm(0, 0)
-        l_col(1, 2)
+        mm(0, 1)
         rs_col(0, 0)
-        l_col(1, 3)
-        softmax(1)
-        mm(0, 1)
+        stat_second(1)
+        mm(0, 2)
+        mm(0, 3)
         rs_col(0, 1)
-        mm(0, 2)
         rs_col(0, 2)
-        stat_second(1)
-        mm(0, 3)
         stat_final(1)
+        make_gl(1)
         loads[4].wait()
-        dp_send()
-        rs_col(0, 3)
-        make_gl(1)
         mm(1, 0)
         mm(1, 1)
         rs_col(1, 0)
+        dp_send()
         mm(1, 2)
+        mm(1, 3)
         rs_col(1, 1)
+        rs_col(1, 2)
+        rs_col(0, 3)
         dp_final()
         finish(0)
-        mm(1, 3)
-        rs_col(1, 2)
         rs_col(1, 3)
         finish(1)
 
@@ -542,6 +565,12 @@
 
 
 NB_TOKENS = 2
+
+
+def write_out(loss, mean, grad, loss_out, mean_out, grad_out):
+    loss_out[...] = loss[...]
+    mean_out[...] = mean[0:1, 0:1]
+    grad_out[...] = grad[...]
 
 
 def shards(hidden_rows, norm_gain, head_weight, teacher_ids, teacher_logits, token_weights):
@@ -565,18 +594,18 @@
         V((NB, TB, VS), F32),
         V((TB, VS), BF16),
         V((T, 8 * K), F32), V((T, 8 * K), F32), V((T, 8 * K), F32), V((T, 8 * K), F32),
-        V((T, 128), F32), V((TB, 128), F32), V((TB, 128), F32),
+        V((T, 128), F32), V((TB, 128), F32), V((4, TB, 128), F32),
         V((NX * NC, 8, 128), F32), V((NZ, 8, 128), F32),
         V((NB, NX * NC, 4 * Q, 128), F32), V((NB, NZ, 4 * Q, 128), F32),
         V((ndp, 8, 128), F32), V((T // 128, 128), F32), V((3, 8, 128), F32),
-        V((4, NZ, NC, FD, TB), F32),
+        V((NB, 4, NZ, NC, FD, TB), F32),
         V((NB, 4, NZ, FD, TB), BF16), V((NB, 4, NZ, FD, TB), BF16),
-        V((NB, 2, 2, FD, TB), BF16), V((NB, 2, 2, FD, TB), BF16),
-        V((NB, 2, 2, 2, FD, TB), BF16), V((NB, 2, 2, 2, FD, TB), BF16),
+        V((NB, 2, NZ, FD // 2, TB), BF16), V((NB, 2, NZ, FD // 2, TB), BF16),
+        V((NB, 2, NZ, FD, TB), BF16), V((NB, 2, NZ, FD, TB), BF16),
         V((NB, NZ, FD, TB), BF16), V((NB, NZ, FD, TB), BF16),
         V((T // 128, 128), F32), V((8, 128), F32), V((FD, T), F32),
-        dma((12,)), dma((NB, 32)), dma((NB, 31)), dma((12,)), dma((10,)),
-        dma((NB, 12)), dma((NB, 10)), dma((ndp,)), dma((ndp,)), dma((NB, 12)), dma((NB, 11)),
+        dma((12,)), dma((NB, 36)), dma((NB, 35)), dma((12,)), dma((10,)),
+        dma((NB, 12)), dma((NB, 10)), dma((ndp,)), dma((ndp,)), dma((NB, 24)), dma((NB, 23)),
     ]
     loss, mean, grad = pl.pallas_call(
         functools.partial(kernel, (NB, TB, VS, ndp, T * ndp)),
@@ -599,7 +628,15 @@
         teacher_logits.T,
         token_weights.reshape(T // 128, 128),
     )
-    return (loss.reshape(T), mean[0, 0], grad.T)
+    loss, mean, grad = pl.pallas_call(
+        write_out,
+        out_shape=(
+            jax.ShapeDtypeStruct((T // 128, 128), F32),
+            jax.ShapeDtypeStruct((1, 1), F32),
+            jax.ShapeDtypeStruct((FD, T), F32),
+        ),
+    )(loss, mean, grad)
+    return (loss.reshape(T), mean.reshape(()), grad.T)
 
 
 def solution(mesh):

time: 85.7 us -> 65.3 us (0.76)
  the two profiles are of different devices: /device:TPU:6 before, /device:TPU:8 now
where the time goes in v2:
time: 65.3 us; the launch traced here: 65.1 us
  Pallas kernels  64.5 us (99%)
    pallas_call x1, Pallas kernels, shards(): pl.pallas_call(functools.partial(kernel, (NB, TB, VS, ndp, T * ndp)), out...  62.9 us
    pallas_call x1, Pallas kernels, shards(): pl.pallas_call(write_out, out_shape=(jax.ShapeDtypeStruct((T // 128, 128)...  1.58 us

profile of v2, /device:TPU:8, one launch (start us, length us, event | category | flops | bytes accessed | tf_op | source)
XLA Modules:
  0.0 65.1 jit_solution(6799490404317127299)
XLA Ops:
  0.6 62.9 %shard_map.85 = (f32[4,128]{1,0:T(4,128)}, f32[8,128]{1,0:T(8,128)}, f32[64,512]{1,0:T(8,128)}) custom-call(f32[64,512]{1,0:T(8,128)} %bitcast.10, f32[16,128]{1,0:T(8,128)} %bitcast.13, bf16[4,4,128,2432]{3,2,1,0:T(8,128)(2,1)} %bitcast.9, s32[32,512]{1,0:T(8,128)} %bitcast.11, f32[32,512]{1,0:T(8,128)} %bitcast.12, f32[4,128]{1,0:T(4,128)} %bitcast.14), custom_call_target="tpu_custom_call" | custom-call | tf_op jit(solution)/shard_map/pallas_call | solution.py:610
  63.6 1.6 %shard_map.86 = (f32[4,128]{1,0:T(4,128)}, f32[1,1]{1,0:T(1,128)}, f32[64,512]{1,0:T(8,128)}) custom-call(f32[4,128]{1,0:T(4,128)} %get-tuple-element.9.loss, f32[8,128]{1,0:T(8,128)} %get-tuple-element.10.mean, f32[64,512]{1,0:T(8,128)} %get-tuple-element.11.grad), custom_call_target="tpu_custom_call" | custom-call | tf_op jit(solution)/shard_map/pallas_call | solution.py:631

commit v3 on v2

--- a/solution.py
+++ b/solution.py
@@ -144,8 +144,8 @@
     def g_half_sem(b, zz, xx, j):
         return gath_r.at[b, at(zz, xx, c) if j == 0 else 32 + zz]
 
-    def g_x(b):
-        for d in (0, 1, 3, 2):
+    def g_x(b, steps=(0, 1, 3, 2)):
+        for d in steps:
             zz = z if d == 0 else zxor(d)
             for j, (src, dst) in enumerate(((xs[2], xs[1]), (xs[1], xs[2]))):
                 g_wait(b, zz, src, c)
@@ -465,56 +465,71 @@
 
     nblk = TB // 8
     if NB == 1:
+        part = nblk // 8
         g_own(0)
         sq_first()
         teacher()
-        targets(0, 0, nblk // 4)
-        g_z(0)
+        targets(0, 0, 2 * part)
+        g_z(0, (1,))
+        g_x(0, (0,))
+        targets(0, 2 * part, 4 * part)
+        g_z(0, (3,))
         sq_second()
-        targets(0, nblk // 4, nblk // 2)
+        g_x(0, (1,))
+        g_z(0, (2,))
+        targets(0, 4 * part, 6 * part)
+        g_x(0, (3,))
         l_col(0, 0)
-        g_x(0)
-        targets(0, nblk // 2, nblk)
+        g_x(0, (2,))
+        targets(0, 6 * part, nblk)
         l_col(0, 1)
+        sq_final()
         g_relay(0)
         l_col(0, 2)
-        sq_final()
         l_col(0, 3)
         softmax(0)
         loads[4].wait()
         stat_second(0)
         stat_final(0)
-        dp_send()
         make_gl(0)
         mm(0, 0)
         mm(0, 1)
         rs_col(0, 0)
         mm(0, 2)
         rs_col(0, 1)
+        rs_col(0, 2)
+        dp_send()
         mm(0, 3)
-        rs_col(0, 2)
         dp_final()
         rs_col(0, 3)
         finish(0)
     else:
+        part = nblk // 4
         g_own(0)
         sq_first()
         g_own(1)
         teacher()
-        targets(0, 0, nblk // 4)
+        targets(0, 0, 2 * part)
         g_z(0, (1,))
-        targets(0, nblk // 4, nblk)
+        g_x(0, (0,))
+        targets(0, 2 * part, 3 * part)
+        g_x(1, (0,))
+        g_z(1, (1,))
+        targets(0, 3 * part, nblk)
+        sq_second()
         g_z(0, (3, 2))
-        sq_second()
-        targets(1, 0, nblk // 2)
-        g_x(0)
+        g_x(0, (1,))
+        targets(1, 0, 2 * part)
+        g_z(1, (3, 2))
+        targets(1, 2 * part, 3 * part)
+        g_x(0, (3, 2))
         l_col(0, 0)
-        g_z(1)
-        targets(1, nblk // 2, nblk)
+        g_x(1, (1,))
+        targets(1, 3 * part, nblk)
         g_relay(0)
         l_col(0, 1)
+        g_x(1, (3, 2))
         l_col(0, 2)
-        g_x(1)
         sq_final()
         l_col(0, 3)
         softmax(0)
@@ -564,7 +579,7 @@
         cp.wait()
 
 
-NB_TOKENS = 2
+NB_TOKENS = 1
 
 
 def write_out(loss, mean, grad, loss_out, mean_out, grad_out):

time: 65.3 us -> 65.2 us (level)
  no operation moved by 1% of the time
where the time goes in v3:
time: 65.2 us; the launch traced here: 65.1 us
  Pallas kernels  64.4 us (99%)
    pallas_call x1, Pallas kernels, shards(): pl.pallas_call(functools.partial(kernel, (NB, TB, VS, ndp, T * ndp)), out...  62.9 us
    pallas_call x1, Pallas kernels, shards(): pl.pallas_call(write_out, out_shape=(jax.ShapeDtypeStruct((T // 128, 128)...  1.58 us

profile of v3, /device:TPU:8, one launch (start us, length us, event | category | flops | bytes accessed | tf_op | source)
XLA Modules:
  0.0 65.1 jit_solution(12942545010338014596)
XLA Ops:
  0.6 62.9 %shard_map.85 = (f32[4,128]{1,0:T(4,128)}, f32[8,128]{1,0:T(8,128)}, f32[64,512]{1,0:T(8,128)}) custom-call(f32[64,512]{1,0:T(8,128)} %bitcast.10, f32[16,128]{1,0:T(8,128)} %bitcast.13, bf16[4,4,128,2432]{3,2,1,0:T(8,128)(2,1)} %bitcast.9, s32[32,512]{1,0:T(8,128)} %bitcast.11, f32[32,512]{1,0:T(8,128)} %bitcast.12, f32[4,128]{1,0:T(4,128)} %bitcast.14), custom_call_target="tpu_custom_call" | custom-call | tf_op jit(solution)/shard_map/pallas_call | solution.py:625
  63.5 1.6 %shard_map.86 = (f32[4,128]{1,0:T(4,128)}, f32[1,1]{1,0:T(1,128)}, f32[64,512]{1,0:T(8,128)}) custom-call(f32[4,128]{1,0:T(4,128)} %get-tuple-element.9.loss, f32[8,128]{1,0:T(8,128)} %get-tuple-element.10.mean, f32[64,512]{1,0:T(8,128)} %get-tuple-element.11.grad), custom_call_target="tpu_custom_call" | custom-call | tf_op jit(solution)/shard_map/pallas_call | solution.py:646

commit v4 on v3

--- a/solution.py
+++ b/solution.py
@@ -479,9 +479,9 @@
         g_z(0, (2,))
         targets(0, 4 * part, 6 * part)
         g_x(0, (3,))
+        targets(0, 6 * part, nblk)
+        g_x(0, (2,))
         l_col(0, 0)
-        g_x(0, (2,))
-        targets(0, 6 * part, nblk)
         l_col(0, 1)
         sq_final()
         g_relay(0)

time: 65.2 us -> 65.1 us (level)
  no operation moved by 1% of the time
where the time goes in v4:
time: 65.1 us; the launch traced here: 65 us
  Pallas kernels  64.4 us (99%)
    pallas_call x1, Pallas kernels, shards(): pl.pallas_call(functools.partial(kernel, (NB, TB, VS, ndp, T * ndp)), out...  62.8 us
    pallas_call x1, Pallas kernels, shards(): pl.pallas_call(write_out, out_shape=(jax.ShapeDtypeStruct((T // 128, 128)...  1.58 us

profile of v4, /device:TPU:8, one launch (start us, length us, event | category | flops | bytes accessed | tf_op | source)
XLA Modules:
  0.0 65.0 jit_solution(16968258464580476762)
XLA Ops:
  0.6 62.8 %shard_map.85 = (f32[4,128]{1,0:T(4,128)}, f32[8,128]{1,0:T(8,128)}, f32[64,512]{1,0:T(8,128)}) custom-call(f32[64,512]{1,0:T(8,128)} %bitcast.10, f32[16,128]{1,0:T(8,128)} %bitcast.13, bf16[4,4,128,2432]{3,2,1,0:T(8,128)(2,1)} %bitcast.9, s32[32,512]{1,0:T(8,128)} %bitcast.11, f32[32,512]{1,0:T(8,128)} %bitcast.12, f32[4,128]{1,0:T(4,128)} %bitcast.14), custom_call_target="tpu_custom_call" | custom-call | tf_op jit(solution)/shard_map/pallas_call | solution.py:625
  63.4 1.6 %shard_map.86 = (f32[4,128]{1,0:T(4,128)}, f32[1,1]{1,0:T(1,128)}, f32[64,512]{1,0:T(8,128)}) custom-call(f32[4,128]{1,0:T(4,128)} %get-tuple-element.9.loss, f32[8,128]{1,0:T(8,128)} %get-tuple-element.10.mean, f32[64,512]{1,0:T(8,128)} %get-tuple-element.11.grad), custom_call_target="tpu_custom_call" | custom-call | tf_op jit(solution)/shard_map/pallas_call | solution.py:646
